TPU v7x, 32 devices: a whole 2x2x4 slice. The times are simulated.
32 devices in a mesh: grp: 4 (over z), lane: 8 (over y, x, core).
Axes of the slice: x: 2, y: 2, z: 4, core: 2. Of those that a mesh axis runs over, the one named last changes fastest.
Arguments:
- tokens: bfloat16 [64, 7168], P('grp', 'lane'), may hold values from -6 to 6
- grad_out: bfloat16 [64, 7168], P('grp', 'lane'), may hold values from -6 to 6
- routes: int32 [64, 2], P('grp'), may hold values from 0 to 3, all different within a row; in each aligned block of 16 rows (0 to 15, 16 to 31, ...) at most 8 rows name the same one
- route_probs: bfloat16 [64, 2], P('grp'), may hold values from 0.049804688 to 1
- gate_weight: bfloat16 [4, 7168, 1024], P('grp', 'lane'), may hold values from -0.0625 to 0.0625
- up_weight: bfloat16 [4, 7168, 1024], P('grp', 'lane'), may hold values from -0.0625 to 0.0625
- down_weight: bfloat16 [4, 1024, 7168], P('grp', None, 'lane'), may hold values from -0.0625 to 0.0625
Outputs:
- token_grad: bfloat16 [64, 7168], P('grp', 'lane')
- prob_grad: bfloat16 [64, 2], P('grp')
- gate_grad: bfloat16 [4, 7168, 1024], P('grp', 'lane')
- up_grad: bfloat16 [4, 7168, 1024], P('grp', 'lane')
- down_grad: bfloat16 [4, 1024, 7168], P('grp', None, 'lane')
Inputs may be any that keep to these rules, and one draw needn't show every extreme that they name: `routes`: each row names 2 different experts. Among the 16 rows of one index of grp (aligned blocks of rows), no expert is named by more than 8 rows, a bound that some block reaches.
All inputs are finite; a program needn't handle non-finite values.
Results may differ from a plain program's by a relative error of at most 0.023.
Values may be sent and summed in bfloat16 or wider, within the bound.
A program may use at most 64 MiB of HBM per device.

v0:
```python
import jax
import jax.numpy as jnp
from jax import lax
from jax.sharding import PartitionSpec as P

MOST = 8


def swiglu_back(gate, upward, grad, weight):
    sig = jax.nn.sigmoid(gate)
    act = gate * sig
    slope = sig * (1.0 + gate * (1.0 - sig))
    hidden = act * upward
    dprob = jnp.sum(hidden * grad, axis=1).astype(jnp.bfloat16)
    dhid = weight[:, None] * grad
    scaled = (weight[:, None] * hidden).astype(jnp.bfloat16)
    d_gate = (dhid * upward * slope).astype(jnp.bfloat16)
    d_up = (dhid * act).astype(jnp.bfloat16)
    return (scaled, d_gate, d_up, dprob)


def shards(tokens, grad_out, routes, route_probs, gate_weight, up_weight, down_weight):
    groups = lax.axis_size("grp")
    lanes = lax.axis_size("lane")
    tok_rows, width = tokens.shape
    fanout = routes.shape[1]
    pairs = tok_rows * fanout
    expert_of = routes.reshape(pairs)
    onehot = (expert_of[:, None] == jnp.arange(groups, dtype=jnp.int32)[None, :]).astype(jnp.int32)
    before = jnp.cumsum(onehot, axis=0) - onehot
    slot_of = jnp.sum(before * onehot, axis=1)
    target = expert_of * MOST + slot_of
    row_count = groups * MOST
    placer = (jnp.arange(row_count, dtype=jnp.int32)[:, None] == target[None, :]).astype(
        jnp.bfloat16
    )
    tok_pairs = jnp.repeat(tokens, fanout, axis=0)
    grad_pairs = jnp.repeat(grad_out, fanout, axis=0)
    send_tok = jnp.dot(placer, tok_pairs, preferred_element_type=jnp.float32).astype(jnp.bfloat16)
    send_grad = jnp.dot(placer, grad_pairs, preferred_element_type=jnp.float32).astype(jnp.bfloat16)
    send_prob = jnp.dot(
        placer, route_probs.reshape(pairs, 1), preferred_element_type=jnp.float32
    ).astype(jnp.bfloat16)
    recv_tok, recv_grad, recv_prob = (
        lax.all_to_all(
            send_tok.reshape(groups, MOST, width), "grp", split_axis=0, concat_axis=0, tiled=True
        ),
        lax.all_to_all(
            send_grad.reshape(groups, MOST, width), "grp", split_axis=0, concat_axis=0, tiled=True
        ),
        lax.all_to_all(
            send_prob.reshape(groups, MOST), "grp", split_axis=0, concat_axis=0, tiled=True
        ),
    )
    rows_tok = recv_tok.reshape(row_count, width)
    rows_grad = recv_grad.reshape(row_count, width)
    rows_prob = recv_prob.reshape(row_count).astype(jnp.float32)
    w_gate = gate_weight[0]
    w_up = up_weight[0]
    w_down = down_weight[0]
    units = w_gate.shape[1]
    share = row_count // lanes
    gate_part = jnp.dot(rows_tok, w_gate, preferred_element_type=jnp.float32)
    up_part = jnp.dot(rows_tok, w_up, preferred_element_type=jnp.float32)
    grad_part = jnp.einsum("rd,ud->ru", rows_grad, w_down, preferred_element_type=jnp.float32)
    summed = lax.psum_scatter(
        jnp.concatenate((gate_part, up_part, grad_part), axis=1).astype(jnp.bfloat16),
        "lane",
        scatter_dimension=0,
        tiled=True,
    ).astype(jnp.float32)
    first = lax.axis_index("lane") * share
    mine = lax.dynamic_slice_in_dim(rows_prob, first, share, 0)
    part_scaled, part_gate, part_up, part_prob = swiglu_back(
        summed[:, :units], summed[:, units : 2 * units], summed[:, 2 * units :], mine
    )
    scaled, d_gate, d_up, dprob = (
        lax.all_gather(part_scaled, "lane", axis=0, tiled=True),
        lax.all_gather(part_gate, "lane", axis=0, tiled=True),
        lax.all_gather(part_up, "lane", axis=0, tiled=True),
        lax.all_gather(part_prob, "lane", axis=0, tiled=True),
    )
    contrib = jnp.einsum("ru,du->rd", d_gate, w_gate, preferred_element_type=jnp.float32)
    contrib = (
        contrib + jnp.einsum("ru,du->rd", d_up, w_up, preferred_element_type=jnp.float32)
    ).astype(jnp.bfloat16)
    gate_grad = jnp.einsum(
        "rd,ru->du", rows_tok, d_gate, preferred_element_type=jnp.float32
    ).astype(jnp.bfloat16)
    up_grad = jnp.einsum("rd,ru->du", rows_tok, d_up, preferred_element_type=jnp.float32).astype(
        jnp.bfloat16
    )
    down_grad = jnp.einsum(
        "ru,rd->ud", scaled, rows_grad, preferred_element_type=jnp.float32
    ).astype(jnp.bfloat16)
    back_tok, back_prob = (
        lax.all_to_all(
            contrib.reshape(groups, MOST, width), "grp", split_axis=0, concat_axis=0, tiled=True
        ),
        lax.all_to_all(dprob.reshape(groups, MOST), "grp", split_axis=0, concat_axis=0, tiled=True),
    )
    picked = jnp.dot(
        placer.T, back_tok.reshape(row_count, width), preferred_element_type=jnp.float32
    )
    token_grad = jnp.sum(picked.reshape(tok_rows, fanout, width), axis=1).astype(jnp.bfloat16)
    prob_grad = jnp.dot(
        placer.T, back_prob.reshape(row_count, 1), preferred_element_type=jnp.float32
    )
    prob_grad = prob_grad.astype(jnp.bfloat16).reshape(tok_rows, fanout)
    return (token_grad, prob_grad, gate_grad[None], up_grad[None], down_grad[None])


def solution(mesh):
    placed = (
        P("grp", "lane"),
        P("grp", "lane"),
        P("grp", None),
        P("grp", None),
        P("grp", "lane", None),
        P("grp", "lane", None),
        P("grp", None, "lane"),
    )
    return jax.shard_map(
        shards,
        mesh=mesh,
        in_specs=placed,
        out_specs=(
            P("grp", "lane"),
            P("grp", None),
            P("grp", "lane", None),
            P("grp", "lane", None),
            P("grp", None, "lane"),
        ),
        check_vma=False,
    )
```

profile of v0, /device:TPU:0, one launch (start us, length us, event | category | flops | bytes accessed | tf_op | source)
XLA Modules:
  0.0 166.9 jit_solution(18149496027524381809)
XLA Ops:
  7.2 0.9 copy.25
  8.5 0.8 broadcast_in_dim.20
  10.1 6.3 %all-to-all-start.1 = ((bf16[4,8,896]{2,1,0:T(8,128)(2,1)}), bf16[4,8,896]{2,1,0:T(8,128)(2,1)S(1)}, u32[]{:S(2)}, u32[]{:S(2)}) async-start(bf16[4,8,896]{2,1,0:T(8,128)(2,1)} %fusion.25), calls=%async_computation.1 | async-start | bytes 114688 | tf_op jit(solution)/shard_map/all_to_all | solution.py:45
  18.9 1.3 fusion.48
  22.3 5.1 %all-to-all-start.2 = ((bf16[4,8,896]{2,1,0:T(8,128)(2,1)}), bf16[4,8,896]{2,1,0:T(8,128)(2,1)S(1)}, u32[]{:S(2)}, u32[]{:S(2)}) async-start(bf16[4,8,896]{2,1,0:T(8,128)(2,1)} %fusion.26), calls=%async_computation.2 | async-start | bytes 114688 | tf_op jit(solution)/shard_map/all_to_all | solution.py:48
  27.8 1.1 copy-done.1
  29.3 3.8 %all-to-all-done.2 = bf16[4,8,896]{2,1,0:T(8,128)(2,1)S(1)} async-done(((bf16[4,8,896]{2,1,0:T(8,128)(2,1)}), bf16[4,8,896]{2,1,0:T(8,128)(2,1)S(1)}, u32[]{:S(2)}, u32[]{:S(2)}) %all-to-all-start.2) | async-done | bytes 57376 | tf_op jit(solution)/shard_map/all_to_all | solution.py:48
  33.1 3.2 %all-to-all-start = ((bf16[4,1,8]{2,1,0:T(2,128)(2,1)}), bf16[4,1,8]{2,1,0:T(2,128)(2,1)S(1)}, u32[]{:S(2)}, u32[]{:S(2)}) async-start(bf16[4,1,8]{2,1,0:T(2,128)(2,1)} %all_to_all.28), calls=%async_computation | async-start | bytes 4096 | tf_op jit(solution)/shard_map/all_to_all | solution.py:51
  36.4 2.1 %fusion.19 = bf16[32,1024]{1,0:T(8,128)(2,1)S(1)} fusion(bf16[1,1024,896]{2,1,0:T(8,128)(2,1)} %param.13, bf16[4,8,896]{2,1,0:T(8,128)(2,1)S(1)} %all-to-all-done.2), kind=kOutput, calls=%fused_computation.16 | convolution fusion | flops 58753024 | bytes 1957888 | tf_op jit(solution)/shard_map/rd,ud->ru/dot_general | solution.py:65
  39.3 2.5 %all-to-all-done = bf16[4,1,8]{2,1,0:T(2,128)(2,1)S(1)} async-done(((bf16[4,1,8]{2,1,0:T(2,128)(2,1)}), bf16[4,1,8]{2,1,0:T(2,128)(2,1)S(1)}, u32[]{:S(2)}, u32[]{:S(2)}) %all-to-all-start) | async-done | bytes 96 | tf_op jit(solution)/shard_map/all_to_all | solution.py:51
  42.0 53.6 %all-reduce.4.cloned.1.call-done = bf16[32,3072]{1,0:T(8,128)(2,1)} async-done(((bf16[32,3072]{1,0:T(8,128)(2,1)}), bf16[32,3072]{1,0:T(8,128)(2,1)}) %all-reduce.4.cloned.1.call-update) | async-done | bytes 196624
  95.6 0.8 dynamic-slice_convert_fusion
  96.9 11.8 %all-reduce = bf16[32]{0:T(256)(128)(2,1)S(1)} all-reduce(bf16[32]{0:T(256)(128)(2,1)S(1)} %dynamic-update-slice), channel_id=1, replica_groups=mesh['grp'=4,'lane'=8] {'lane'}, use_global_device_ids=true, to_apply=%add | all-reduce | flops 32 | bytes 128
  109.4 4.6 %all-to-all-start.4 = ((bf16[4,1,8]{2,1,0:T(2,128)(2,1)}), bf16[4,1,8]{2,1,0:T(2,128)(2,1)S(1)}, u32[]{:S(2)}, u32[]{:S(2)}) async-start(bf16[4,1,8]{2,1,0:T(2,128)(2,1)} %all_to_all.29), calls=%async_computation.4 | async-start | bytes 4096 | tf_op jit(solution)/shard_map/all_to_all | solution.py:100
  114.0 8.6 %all-gather.2 = bf16[8,4,1024]{2,1,0:T(4,128)(2,1)S(1)} all-gather(bf16[1,4,1024]{2,1,0:T(4,128)(2,1)S(1)} %get-tuple-element.25), channel_id=1, replica_groups=mesh['grp'=4,'lane'=8] {'lane'}, dimensions={0}, use_global_device_ids=true | all-gather | bytes 73728 | tf_op jit(solution)/shard_map/all_gather | solution.py:78
  122.6 8.9 %all-gather.1 = bf16[8,4,1024]{2,1,0:T(4,128)(2,1)S(1)} all-gather(bf16[1,4,1024]{2,1,0:T(4,128)(2,1)S(1)} %get-tuple-element.26), channel_id=1, replica_groups=mesh['grp'=4,'lane'=8] {'lane'}, dimensions={0}, use_global_device_ids=true | all-gather | bytes 73728 | tf_op jit(solution)/shard_map/all_gather | solution.py:80
  131.5 8.6 %all-gather = bf16[8,4,1024]{2,1,0:T(4,128)(2,1)S(1)} all-gather(bf16[1,4,1024]{2,1,0:T(4,128)(2,1)S(1)} %get-tuple-element.27), channel_id=1, replica_groups=mesh['grp'=4,'lane'=8] {'lane'}, dimensions={0}, use_global_device_ids=true | all-gather | bytes 73728 | tf_op jit(solution)/shard_map/all_gather | solution.py:79
  140.7 0.9 copy-done.2
  141.6 1.3 fusion.27
  142.9 1.9 %convert_bitcast_fusion.2 = bf16[1,896,1024]{2,1,0:T(8,128)(2,1)} fusion(bf16[32,1024]{1,0:T(8,128)(2,1)S(1)} %reshape.122, bf16[4,8,896]{2,1,0:T(8,128)(2,1)S(1)} %all-to-all-done.1), kind=kOutput, calls=%fused_computation.12 | convolution fusion | flops 59637760 | bytes 1957888 | tf_op jit(solution)/shard_map/rd,ru->du/dot_general | solution.py:87
  144.7 1.9 %convert_bitcast_fusion.1 = bf16[1,896,1024]{2,1,0:T(8,128)(2,1)} fusion(bf16[32,1024]{1,0:T(8,128)(2,1)S(1)} %reshape.124, bf16[4,8,896]{2,1,0:T(8,128)(2,1)S(1)} %all-to-all-done.1), kind=kOutput, calls=%fused_computation.11 | convolution fusion | flops 59637760 | bytes 1957888 | tf_op jit(solution)/shard_map/rd,ru->du/dot_general | solution.py:90
  146.6 1.9 %convert_bitcast_fusion = bf16[1,1024,896]{2,1,0:T(8,128)(2,1)} fusion(bf16[32,1024]{1,0:T(8,128)(2,1)S(1)} %reshape.126, bf16[4,8,896]{2,1,0:T(8,128)(2,1)S(1)} %all-to-all-done.2), kind=kOutput, calls=%fused_computation.10 | convolution fusion | flops 59637760 | bytes 1957888 | tf_op jit(solution)/shard_map/ru,rd->ud/dot_general | solution.py:93
  148.5 5.1 %all-to-all-start.3 = ((bf16[4,8,896]{2,1,0:T(8,128)(2,1)}), bf16[4,8,896]{2,1,0:T(8,128)(2,1)S(1)}, u32[]{:S(2)}, u32[]{:S(2)}) async-start(bf16[4,8,896]{2,1,0:T(8,128)(2,1)} %fusion.27), calls=%async_computation.3 | async-start | bytes 114688 | tf_op jit(solution)/shard_map/all_to_all | solution.py:97
  154.6 4.8 %all-to-all-done.3 = bf16[4,8,896]{2,1,0:T(8,128)(2,1)S(1)} async-done(((bf16[4,8,896]{2,1,0:T(8,128)(2,1)}), bf16[4,8,896]{2,1,0:T(8,128)(2,1)S(1)}, u32[]{:S(2)}, u32[]{:S(2)}) %all-to-all-start.3) | async-done | bytes 57376 | tf_op jit(solution)/shard_map/all_to_all | solution.py:97
  (44 shorter events, 9.8 us)
Async XLA Ops:
  7.2 20.3 %copy-start = (bf16[1,896,1024]{2,1,0:T(8,128)(2,1)S(1)}, bf16[1,896,1024]{2,1,0:T(8,128)(2,1)}, u32[]{:S(2)}) copy-start(bf16[1,896,1024]{2,1,0:T(8,128)(2,1)} %param.12) | copy-start | bytes 5505028
  10.1 12.3 %all-to-all-start.1 = ((bf16[4,8,896]{2,1,0:T(8,128)(2,1)}), bf16[4,8,896]{2,1,0:T(8,128)(2,1)S(1)}, u32[]{:S(2)}, u32[]{:S(2)}) async-start(bf16[4,8,896]{2,1,0:T(8,128)(2,1)} %fusion.25), calls=%async_computation.1 | async-start | bytes 114688 | tf_op jit(solution)/shard_map/all_to_all | solution.py:45
  22.3 10.8 %all-to-all-start.2 = ((bf16[4,8,896]{2,1,0:T(8,128)(2,1)}), bf16[4,8,896]{2,1,0:T(8,128)(2,1)S(1)}, u32[]{:S(2)}, u32[]{:S(2)}) async-start(bf16[4,8,896]{2,1,0:T(8,128)(2,1)} %fusion.26), calls=%async_computation.2 | async-start | bytes 114688 | tf_op jit(solution)/shard_map/all_to_all | solution.py:48
  27.4 1.5 copy-start.1
  33.1 8.7 %all-to-all-start = ((bf16[4,1,8]{2,1,0:T(2,128)(2,1)}), bf16[4,1,8]{2,1,0:T(2,128)(2,1)S(1)}, u32[]{:S(2)}, u32[]{:S(2)}) async-start(bf16[4,1,8]{2,1,0:T(2,128)(2,1)} %all_to_all.28), calls=%async_computation | async-start | bytes 4096 | tf_op jit(solution)/shard_map/all_to_all | solution.py:51
  36.4 59.3 %all-reduce.4.cloned.1.call-start = ((), (), s32[]{:S(2)}) async-start(), calls=%async_computation.5 | async-start | bytes 393216
  109.4 39.1 %all-to-all-start.4 = ((bf16[4,1,8]{2,1,0:T(2,128)(2,1)}), bf16[4,1,8]{2,1,0:T(2,128)(2,1)S(1)}, u32[]{:S(2)}, u32[]{:S(2)}) async-start(bf16[4,1,8]{2,1,0:T(2,128)(2,1)} %all_to_all.29), calls=%async_computation.4 | async-start | bytes 4096 | tf_op jit(solution)/shard_map/all_to_all | solution.py:100
  140.1 1.5 copy-start.2
  148.5 10.8 %all-to-all-start.3 = ((bf16[4,8,896]{2,1,0:T(8,128)(2,1)}), bf16[4,8,896]{2,1,0:T(8,128)(2,1)S(1)}, u32[]{:S(2)}, u32[]{:S(2)}) async-start(bf16[4,8,896]{2,1,0:T(8,128)(2,1)} %fusion.27), calls=%async_computation.3 | async-start | bytes 114688 | tf_op jit(solution)/shard_map/all_to_all | solution.py:97
Sparse Core Ops, SparseCore 0:
  40.8 54.7 all-reduce.3
where the time goes:
time: 168 us; the launch traced here: 167 us
  waiting for transfers between devices  64.8 us (39%)
  blocking collectives  37.9 us (23%)
  starting transfers between devices  24.4 us (15%)
  between operations  15.4 us (9%)
  matrix products  13.1 us (8%)
  local copies, waits for them, and re-layouts  9.32 us (6%)
  other arithmetic  2.12 us (1%)
    unnamed x2, waiting for transfers between devices  53.7 us
    unnamed x1, blocking collectives  11.8 us
    all_gather x1, blocking collectives, shards(): lax.all_gather(part_up, 'lane', axis=0, tiled=True)  8.88 us
    all_gather x1, blocking collectives, shards(): lax.all_gather(part_gate, 'lane', axis=0, tiled=True)  8.59 us
    all_gather x1, blocking collectives, shards(): lax.all_gather(part_scaled, 'lane', axis=0, tiled=True)  8.57 us
    all_to_all x1, starting transfers between devices, shards(): lax.all_to_all(send_tok.reshape(groups, MOST, width), 'grp', split_axis=0...  6.32 us
    unnamed x15, local copies, waits for them, and re-layouts  5.82 us
    all_to_all x1, starting transfers between devices, shards(): lax.all_to_all(send_grad.reshape(groups, MOST, width), 'grp', split_axis=...  5.09 us
  transfers between devices with their start and end apart: 6, of which 4 were waited for; matrix products, arithmetic and copies ran while one was open for 10% of the time, Pallas kernels for 0%

commit v1 on v0

--- a/solution.py
+++ b/solution.py
@@ -1,9 +1,14 @@
+import functools
+
 import jax
 import jax.numpy as jnp
 from jax import lax
+from jax.experimental import pallas as pl
+from jax.experimental.pallas import tpu as pltpu
 from jax.sharding import PartitionSpec as P
 
 MOST = 8
+MESH = pl.DeviceIdType.MESH
 
 
 def swiglu_back(gate, upward, grad, weight):
@@ -19,7 +24,7 @@
     return (scaled, d_gate, d_up, dprob)
 
 
-def shards(tokens, grad_out, routes, route_probs, gate_weight, up_weight, down_weight):
+def plain_shards(tokens, grad_out, routes, route_probs, gate_weight, up_weight, down_weight):
     groups = lax.axis_size("grp")
     lanes = lax.axis_size("lane")
     tok_rows, width = tokens.shape
@@ -110,6 +115,348 @@
     return (token_grad, prob_grad, gate_grad[None], up_grad[None], down_grad[None])
 
 
+def tn_dot(a, b):
+    return lax.dot_general(a, b, (((0,), (0,)), ((), ())), preferred_element_type=jnp.float32)
+
+
+def nt_dot(a, b):
+    return lax.dot_general(a, b, (((1,), (1,)), ((), ())), preferred_element_type=jnp.float32)
+
+
+def fused(
+    groups,
+    lanes,
+    tok_ref,
+    cot_ref,
+    routes_ref,
+    probs_ref,
+    wg_hbm,
+    wu_hbm,
+    wd_hbm,
+    tg_ref,
+    pg_ref,
+    gg_hbm,
+    ug_hbm,
+    dg_hbm,
+    wg,
+    wu,
+    wd,
+    gg,
+    ug,
+    dg,
+    send_a,
+    recv_a,
+    send_rs,
+    recv_rs,
+    gat,
+    send_b,
+    recv_b,
+    win_sem,
+    wout_sem,
+    sa_sem,
+    ra_sem,
+    ss_sem,
+    rs_sem,
+    sg_sem,
+    rg_sem,
+    sb_sem,
+    rb_sem,
+):
+    f32, bf16 = jnp.float32, jnp.bfloat16
+    g_me = lax.axis_index("grp")
+    l_me = lax.axis_index("lane")
+    tok_rows, width = tok_ref.shape
+    fanout = routes_ref.shape[1]
+    units = wg.shape[1]
+    chunk = units // lanes
+    rows = groups * MOST
+    left = send_b.shape[2]
+    grp_peers = [lax.rem(g_me + j, groups) for j in range(1, groups)]
+    lane_peers = [lax.rem(l_me + j, lanes) for j in range(1, lanes)]
+
+    barrier = pltpu.get_barrier_semaphore()
+    for g in grp_peers:
+        pl.semaphore_signal(barrier, inc=1, device_id=(g, l_me), device_id_type=MESH)
+    for l in lane_peers:
+        pl.semaphore_signal(barrier, inc=1, device_id=(g_me, l), device_id_type=MESH)
+
+    loads = [
+        pltpu.make_async_copy(wg_hbm.at[0], wg, win_sem.at[0]),
+        pltpu.make_async_copy(wu_hbm.at[0], wu, win_sem.at[1]),
+        pltpu.make_async_copy(wd_hbm.at[0], wd, win_sem.at[2]),
+    ]
+    for load in loads:
+        load.start()
+
+    r_wide = routes_ref[...]
+    p_wide = probs_ref[...].astype(f32)
+    t_row = lax.broadcasted_iota(jnp.int32, (tok_rows, tok_rows), 0)
+    t_col = lax.broadcasted_iota(jnp.int32, (tok_rows, tok_rows), 1)
+    eye = t_row == t_col
+    row_id = lax.broadcasted_iota(jnp.int32, (rows, tok_rows), 0)
+    col_id = lax.broadcasted_iota(jnp.int32, (tok_rows, rows), 1)
+    row_exp, row_slot = row_id // MOST, row_id % MOST
+    col_exp, col_slot = col_id // MOST, col_id % MOST
+    named = jnp.zeros((rows, tok_rows), f32)
+    chance = jnp.zeros((rows, tok_rows), f32)
+    named_t = jnp.zeros((tok_rows, rows), f32)
+    hits = []
+    for k in range(fanout):
+        r_col = r_wide[:, k : k + 1].astype(f32)
+        p_col = p_wide[:, k : k + 1]
+        r_lane = jnp.sum(jnp.where(eye, r_col, 0.0), axis=0, keepdims=True)
+        p_lane = jnp.sum(jnp.where(eye, p_col, 0.0), axis=0, keepdims=True)
+        hit = (row_exp.astype(f32) == r_lane).astype(f32)
+        named = named + hit
+        chance = chance + hit * p_lane
+        hit_t = (col_exp.astype(f32) == r_col).astype(f32)
+        named_t = named_t + hit_t
+        hits.append(hit_t)
+    before = jnp.dot(
+        named.astype(bf16), (t_row < t_col).astype(bf16), preferred_element_type=f32
+    )
+    before_t = jnp.dot(
+        (t_col < t_row).astype(bf16), named_t.astype(bf16), preferred_element_type=f32
+    )
+    placer = jnp.where(before == row_slot.astype(f32), named, 0.0)
+    placer_t = jnp.where(before_t == col_slot.astype(f32), named_t, 0.0)
+    row_prob = jnp.sum(placer * chance, axis=1, keepdims=True)
+    placed = placer.astype(bf16)
+    out_tok = jnp.dot(placed, tok_ref[...], preferred_element_type=f32)
+    out_cot = jnp.dot(placed, cot_ref[...], preferred_element_type=f32)
+    prob_tile = jnp.broadcast_to(row_prob, (rows, chunk))
+    for e in range(groups):
+        at = slice(e * MOST, (e + 1) * MOST)
+        send_a[e, :, :width] = jnp.concatenate((out_tok[at], out_cot[at]), axis=0).astype(bf16)
+        send_a[e, :, width:] = jnp.concatenate((prob_tile[at], prob_tile[at]), axis=0).astype(bf16)
+
+    pl.semaphore_wait(barrier, groups + lanes - 2)
+
+    def a_copy(to, slot):
+        return pltpu.make_async_remote_copy(
+            src_ref=send_a.at[to],
+            dst_ref=recv_a.at[slot],
+            send_sem=sa_sem.at[to],
+            recv_sem=ra_sem.at[slot],
+            device_id=(to, l_me),
+            device_id_type=MESH,
+        )
+
+    for g in grp_peers:
+        a_copy(g, g_me).start()
+    recv_a[g_me] = send_a[g_me]
+    for load in loads:
+        load.wait()
+    for g in grp_peers:
+        a_copy(g, g).wait_recv()
+
+    tok_in, cot_in, prob_in = [], [], []
+    for g in range(groups):
+        both = recv_a[g].astype(f32)
+        tok_in.append(both[:MOST, :width])
+        cot_in.append(both[MOST:, :width])
+        prob_in.append(both[:MOST, width:])
+    rows_tok = jnp.concatenate(tok_in, axis=0).astype(bf16)
+    rows_cot = jnp.concatenate(cot_in, axis=0).astype(bf16)
+    prob = jnp.concatenate(prob_in, axis=0)
+
+    def rs_copy(to, slot):
+        return pltpu.make_async_remote_copy(
+            src_ref=send_rs.at[to],
+            dst_ref=recv_rs.at[slot],
+            send_sem=ss_sem.at[to],
+            recv_sem=rs_sem.at[slot],
+            device_id=(g_me, to),
+            device_id_type=MESH,
+        )
+
+    chips = lanes // 2
+    chip_me, core_me = l_me // 2, l_me % 2
+    for j in range(1, chips + 1):
+        chip = lax.rem(chip_me + j, chips)
+        at = pl.ds(pl.multiple_of(chip * (2 * chunk), 2 * chunk), 2 * chunk)
+        parts = (
+            jnp.dot(rows_tok, wg[:, at], preferred_element_type=f32).astype(bf16),
+            jnp.dot(rows_tok, wu[:, at], preferred_element_type=f32).astype(bf16),
+            nt_dot(rows_cot, wd[at, :]).astype(bf16),
+        )
+        for h in range(2):
+            for i, part in enumerate(parts):
+                send_rs[2 * chip + h, :, i * chunk : (i + 1) * chunk] = part[
+                    :, h * chunk : (h + 1) * chunk
+                ]
+            if j < chips:
+                rs_copy(2 * chip + h, l_me).start()
+    rs_copy(2 * chip_me + 1 - core_me, l_me).start()
+    recv_rs[l_me] = send_rs[l_me]
+    for l in lane_peers:
+        rs_copy(l, l).wait_recv()
+
+    summed = recv_rs[0].astype(f32)
+    for l in range(1, lanes):
+        summed = summed + recv_rs[l].astype(f32)
+    gate, upward, grad = (summed[:, i * chunk : (i + 1) * chunk] for i in range(3))
+    sig = jax.nn.sigmoid(gate)
+    act = gate * sig
+    slope = sig * (1.0 + gate * (1.0 - sig))
+    hidden = act * upward
+    dpart = jnp.sum(hidden * grad, axis=1, keepdims=True)
+    dhid = prob * grad
+    gat[l_me, :, :chunk] = (dhid * upward * slope).astype(bf16)
+    gat[l_me, :, chunk : 2 * chunk] = (dhid * act).astype(bf16)
+    gat[l_me, :, 2 * chunk : 3 * chunk] = (prob * hidden).astype(bf16)
+    high = dpart.astype(bf16).astype(f32)
+    lane_id = lax.broadcasted_iota(jnp.int32, (rows, chunk), 1)
+    gat[l_me, :, 3 * chunk :] = jnp.where(lane_id < chunk // 2, high, dpart - high).astype(bf16)
+
+    def ag_copy(to, slot):
+        return pltpu.make_async_remote_copy(
+            src_ref=gat.at[slot],
+            dst_ref=gat.at[slot],
+            send_sem=sg_sem.at[to],
+            recv_sem=rg_sem.at[slot],
+            device_id=(g_me, to),
+            device_id_type=MESH,
+        )
+
+    for l in lane_peers:
+        ag_copy(l, l_me).start()
+    for l in lane_peers:
+        ag_copy(l, l).wait_recv()
+
+    d_gate = jnp.concatenate([gat[l, :, :chunk] for l in range(lanes)], axis=1)
+    d_up = jnp.concatenate([gat[l, :, chunk : 2 * chunk] for l in range(lanes)], axis=1)
+    scaled = jnp.concatenate([gat[l, :, 2 * chunk : 3 * chunk] for l in range(lanes)], axis=1)
+    dtile = gat[0, :, 3 * chunk :].astype(f32)
+    for l in range(1, lanes):
+        dtile = dtile + gat[l, :, 3 * chunk :].astype(f32)
+    dprob = jnp.sum(dtile, axis=1, keepdims=True) * (2.0 / chunk)
+    dprob = jnp.broadcast_to(dprob, (rows, 128))
+
+    contrib = nt_dot(d_gate, wg[...]) + nt_dot(d_up, wu[...])
+    for e in range(groups):
+        at = slice(e * MOST, (e + 1) * MOST)
+        right = jnp.concatenate((contrib[at, left:], dprob[at]), axis=1)
+        pad = left - right.shape[1]
+        if pad:
+            right = jnp.concatenate((right, jnp.zeros((MOST, pad), f32)), axis=1)
+        send_b[e] = jnp.concatenate((contrib[at, :left], right), axis=0).astype(bf16)
+
+    def b_copy(to, slot):
+        return pltpu.make_async_remote_copy(
+            src_ref=send_b.at[to],
+            dst_ref=recv_b.at[slot],
+            send_sem=sb_sem.at[to],
+            recv_sem=rb_sem.at[slot],
+            device_id=(to, l_me),
+            device_id_type=MESH,
+        )
+
+    for g in grp_peers:
+        b_copy(g, g_me).start()
+    recv_b[g_me] = send_b[g_me]
+
+    stores = [
+        pltpu.make_async_copy(gg, gg_hbm.at[0], wout_sem.at[0]),
+        pltpu.make_async_copy(ug, ug_hbm.at[0], wout_sem.at[1]),
+        pltpu.make_async_copy(dg, dg_hbm.at[0], wout_sem.at[2]),
+    ]
+    gg[...] = tn_dot(rows_tok, d_gate).astype(bf16)
+    stores[0].start()
+    ug[...] = tn_dot(rows_tok, d_up).astype(bf16)
+    stores[1].start()
+    dg[...] = tn_dot(scaled, rows_cot).astype(bf16)
+    stores[2].start()
+
+    for g in grp_peers:
+        b_copy(g, g).wait_recv()
+    low, top = [], []
+    for g in range(groups):
+        both = recv_b[g].astype(f32)
+        low.append(both[:MOST])
+        top.append(both[MOST:])
+    low = jnp.concatenate(low, axis=0).astype(bf16)
+    top = jnp.concatenate(top, axis=0).astype(bf16)
+    back = placer_t.astype(bf16)
+    tg_ref[:, :left] = jnp.dot(back, low, preferred_element_type=f32).astype(bf16)
+    tg_ref[:, left:] = jnp.dot(
+        back, top[:, : width - left], preferred_element_type=f32
+    ).astype(bf16)
+    dback = top[:, width - left : width - left + 128]
+    pick = lax.broadcasted_iota(jnp.int32, (tok_rows, 128), 1)
+    result = jnp.zeros((tok_rows, 128), f32)
+    for k in range(fanout):
+        mine = jnp.dot((placer_t * hits[k]).astype(bf16), dback, preferred_element_type=f32)
+        result = jnp.where(pick == k, mine, result)
+    pg_ref[...] = result[:, :fanout].astype(bf16)
+
+    for g in grp_peers:
+        a_copy(g, g_me).wait_send()
+        b_copy(g, g_me).wait_send()
+    for l in lane_peers:
+        rs_copy(l, l_me).wait_send()
+        ag_copy(l, l_me).wait_send()
+    for store in stores:
+        store.wait()
+
+
+def shards(tokens, grad_out, routes, route_probs, gate_weight, up_weight, down_weight):
+    groups = lax.axis_size("grp")
+    lanes = lax.axis_size("lane")
+    tok_rows, width = tokens.shape
+    units = gate_weight.shape[2]
+    chunk = units // lanes
+    args = (tokens, grad_out, routes, route_probs, gate_weight, up_weight, down_weight)
+    if width % 128 or chunk % 128 or lanes % 2 or tok_rows % 16:
+        return plain_shards(*args)
+    rows = groups * MOST
+    left = 128 * ((width // 128 + 2) // 2)
+    bf16 = jnp.bfloat16
+    vmem = pl.BlockSpec(memory_space=pltpu.VMEM)
+    hbm = pl.BlockSpec(memory_space=pl.ANY)
+    dma = pltpu.SemaphoreType.DMA
+    return pl.pallas_call(
+        functools.partial(fused, groups, lanes),
+        out_shape=(
+            jax.ShapeDtypeStruct(tokens.shape, bf16),
+            jax.ShapeDtypeStruct(route_probs.shape, bf16),
+            jax.ShapeDtypeStruct(gate_weight.shape, bf16),
+            jax.ShapeDtypeStruct(up_weight.shape, bf16),
+            jax.ShapeDtypeStruct(down_weight.shape, bf16),
+        ),
+        in_specs=[vmem] * 4 + [hbm] * 3,
+        out_specs=(vmem, vmem, hbm, hbm, hbm),
+        scratch_shapes=[
+            pltpu.VMEM((width, units), bf16),
+            pltpu.VMEM((width, units), bf16),
+            pltpu.VMEM((units, width), bf16),
+            pltpu.VMEM((width, units), bf16),
+            pltpu.VMEM((width, units), bf16),
+            pltpu.VMEM((units, width), bf16),
+            pltpu.VMEM((groups, 2 * MOST, width + chunk), bf16),
+            pltpu.VMEM((groups, 2 * MOST, width + chunk), bf16),
+            pltpu.VMEM((lanes, rows, 3 * chunk), bf16),
+            pltpu.VMEM((lanes, rows, 3 * chunk), bf16),
+            pltpu.VMEM((lanes, rows, 4 * chunk), bf16),
+            pltpu.VMEM((groups, 2 * MOST, left), bf16),
+            pltpu.VMEM((groups, 2 * MOST, left), bf16),
+            dma((3,)),
+            dma((3,)),
+            dma((groups,)),
+            dma((groups,)),
+            dma((lanes,)),
+            dma((lanes,)),
+            dma((lanes,)),
+            dma((lanes,)),
+            dma((groups,)),
+            dma((groups,)),
+        ],
+        compiler_params=pltpu.CompilerParams(
+            collective_id=0, has_side_effects=True, vmem_limit_bytes=48 * 1024 * 1024
+        ),
+    )(*args)
+
+
 def solution(mesh):
     placed = (
         P("grp", "lane"),

time: 168 us -> 38.1 us (0.23)
  waiting for transfers between devices: 64.8 us -> 0 us
  blocking collectives: 37.9 us -> 0 us
  Pallas kernels: 0 us -> 25 us
  starting transfers between devices: 24.4 us -> 0 us
  between operations: 15.4 us -> 0.65 us
  matrix products: 13.1 us -> 0 us
  local copies, waits for them, and re-layouts: 9.32 us -> 12.1 us
  other arithmetic: 2.12 us -> 0 us
    unnamed x2 -> x0, waiting for transfers between devices: 53.7 us -> none
    all_gather x3 -> x0, blocking collectives: 26 us -> none  [the longest x1 8.88 us: shards(): lax.all_gather(part_up, 'lane', axis=0, tiled=True)]
    pallas_call x0 -> x1, Pallas kernels: none -> 25 us  [shards(): pl.pallas_call(functools.partial(fused, groups, lanes), out_shape=(jax.Sh...]
    all_to_all x5 -> x0, starting transfers between devices: 24.3 us -> none  [the longest x1 6.32 us: shards(): lax.all_to_all(send_tok.reshape(groups, MOST, width), 'grp', split_axis=0...]
    dot_general x13 -> x0, matrix products: 13.1 us -> none  [the longest x1 2.12 us: shards(): jnp.einsum('rd,ud->ru', rows_grad, w_down, preferred_element_type=jnp.flo...]
    unnamed x1 -> x0, blocking collectives: 11.8 us -> none
    all_to_all x5 -> x0, waiting for transfers between devices: 11.1 us -> none  [the longest x1 4.78 us: shards(): lax.all_to_all(contrib.reshape(groups, MOST, width), 'grp', split_axis=0,...]
    unnamed x15 -> x16, local copies, waits for them, and re-layouts: 5.82 us -> 11.5 us
  transfers between devices with their start and end apart: 6 -> 0, of which waited for: 4 -> 0; matrix products, arithmetic and copies ran while one was open for 10% -> 0% of each run, Pallas kernels for 0% -> 0%
where the time goes in v1:
time: 38.1 us; the launch traced here: 37.8 us
  Pallas kernels  25 us (66%)
  local copies, waits for them, and re-layouts  12.1 us (32%)
  between operations  0.65 us (2%)
    pallas_call x1, Pallas kernels, shards(): pl.pallas_call(functools.partial(fused, groups, lanes), out_shape=(jax.Sh...  25 us
    unnamed x16, local copies, waits for them, and re-layouts  11.5 us

profile of v1, /device:TPU:0, one launch (start us, length us, event | category | flops | bytes accessed | tf_op | source)
XLA Modules:
  0.0 37.8 jit_solution(9663808127521642176)
XLA Ops:
  0.6 0.7 %copy.13.probs_ref = bf16[16,2]{1,0:T(8,128)(2,1)S(1)} copy(bf16[16,2]{0,1:T(2,128)(2,1)} %param.10) | data formatting | bytes 128 | tf_op args[3]
  1.4 0.8 %copy.12.routes_ref = s32[16,2]{1,0:T(8,128)S(1)} copy(s32[16,2]{0,1:T(2,128)} %param.9) | data formatting | bytes 256 | tf_op args[2]
  2.1 0.0 copy-start.3
  2.1 0.7 %copy-done.3 = bf16[16,896]{1,0:T(8,128)(2,1)S(1)} copy-done((bf16[16,896]{1,0:T(8,128)(2,1)S(1)}, bf16[16,896]{1,0:T(8,128)(2,1)}, u32[]{:S(2)}) %copy-start.3) | copy-done | bytes 28696
  2.9 0.0 copy-start.4
  2.9 0.7 %copy-done.4 = bf16[16,896]{1,0:T(8,128)(2,1)S(1)} copy-done((bf16[16,896]{1,0:T(8,128)(2,1)S(1)}, bf16[16,896]{1,0:T(8,128)(2,1)}, u32[]{:S(2)}) %copy-start.4) | copy-done | bytes 28696
  3.6 25.0 %shard_map.110 = (bf16[16,896]{1,0:T(8,128)(2,1)S(1)}, bf16[16,2]{1,0:T(8,128)(2,1)S(1)}, bf16[1,896,1024]{2,1,0:T(8,128)(2,1)S(1)}, bf16[1,896,1024]{2,1,0:T(8,128)(2,1)S(1)}, bf16[1,1024,896]{2,1,0:T(8,128)(2,1)S(1)}) custom-call(bf16[16,896]{1,0:T(8,128)(2,1)S(1)} %copy-done.3, bf16[16,896]{1,0:T(8,128)(2,1)S(1)} %copy-done.4, ...), custom_call_target="tpu_custom_call" | custom-call | tf_op jit(solution)/shard_map/pallas_call | solution.py:418
  28.7 0.0 copy-start
  28.7 1.2 %copy-done = bf16[1,896,1024]{2,1,0:T(8,128)(2,1)} copy-done((bf16[1,896,1024]{2,1,0:T(8,128)(2,1)}, bf16[1,896,1024]{2,1,0:T(8,128)(2,1)S(1)}, u32[]{:S(2)}) %copy-start) | copy-done | bytes 1835032
  29.9 0.0 copy-start.2
  29.9 1.2 %copy-done.2 = bf16[1,896,1024]{2,1,0:T(8,128)(2,1)} copy-done((bf16[1,896,1024]{2,1,0:T(8,128)(2,1)}, bf16[1,896,1024]{2,1,0:T(8,128)(2,1)S(1)}, u32[]{:S(2)}) %copy-start.2) | copy-done | bytes 1835032
  31.1 0.6 %copy.14 = bf16[16,2]{0,1:T(2,128)(2,1)} copy(bf16[16,2]{1,0:T(8,128)(2,1)S(1)} %get-tuple-element.6) | data formatting | bytes 128 | tf_op jit(solution)/shard_map/pallas_call | solution.py:418
  31.7 0.6 %copy.19 = bf16[16,896]{1,0:T(8,128)(2,1)} copy(bf16[16,896]{1,0:T(8,128)(2,1)S(1)} %get-tuple-element.15) | data formatting | bytes 57344
  32.3 0.0 copy-start.1
  32.3 3.0 %copy.20 = bf16[1,896,1024]{2,1,0:T(8,128)(2,1)} copy(bf16[1,896,1024]{2,1,0:T(8,128)(2,1)} %copy-done.2) | data formatting | bytes 3670016
  35.3 0.0 copy-done.1
  35.3 1.2 %copy.21 = bf16[1,896,1024]{2,1,0:T(8,128)(2,1)} copy(bf16[1,896,1024]{2,1,0:T(8,128)(2,1)S(1)} %copy-done.1) | data formatting | bytes 3670016
  36.6 1.2 %copy.22 = bf16[1,1024,896]{2,1,0:T(8,128)(2,1)} copy(bf16[1,1024,896]{2,1,0:T(8,128)(2,1)S(1)} %get-tuple-element.19) | data formatting | bytes 3670016
Async XLA Ops:
  2.1 0.7 %copy-start.3 = (bf16[16,896]{1,0:T(8,128)(2,1)S(1)}, bf16[16,896]{1,0:T(8,128)(2,1)}, u32[]{:S(2)}) copy-start(bf16[16,896]{1,0:T(8,128)(2,1)} %tok_ref.1) | copy-start | bytes 86020
  2.9 0.7 %copy-start.4 = (bf16[16,896]{1,0:T(8,128)(2,1)S(1)}, bf16[16,896]{1,0:T(8,128)(2,1)}, u32[]{:S(2)}) copy-start(bf16[16,896]{1,0:T(8,128)(2,1)} %cot_ref.1) | copy-start | bytes 86020
  28.7 1.2 %copy-start = (bf16[1,896,1024]{2,1,0:T(8,128)(2,1)}, bf16[1,896,1024]{2,1,0:T(8,128)(2,1)S(1)}, u32[]{:S(2)}) copy-start(bf16[1,896,1024]{2,1,0:T(8,128)(2,1)S(1)} %get-tuple-element.18) | copy-start | bytes 5505028
  29.9 1.2 %copy-start.2 = (bf16[1,896,1024]{2,1,0:T(8,128)(2,1)}, bf16[1,896,1024]{2,1,0:T(8,128)(2,1)S(1)}, u32[]{:S(2)}) copy-start(bf16[1,896,1024]{2,1,0:T(8,128)(2,1)S(1)} %get-tuple-element.17) | copy-start | bytes 5505028
  32.3 3.0 %copy-start.1 = (bf16[1,896,1024]{2,1,0:T(8,128)(2,1)S(1)}, bf16[1,896,1024]{2,1,0:T(8,128)(2,1)}, u32[]{:S(2)}) copy-start(bf16[1,896,1024]{2,1,0:T(8,128)(2,1)} %copy-done) | copy-start | bytes 5505028

commit v2 on v1

--- a/solution.py
+++ b/solution.py
@@ -115,10 +115,6 @@
     return (token_grad, prob_grad, gate_grad[None], up_grad[None], down_grad[None])
 
 
-def tn_dot(a, b):
-    return lax.dot_general(a, b, (((0,), (0,)), ((), ())), preferred_element_type=jnp.float32)
-
-
 def nt_dot(a, b):
     return lax.dot_general(a, b, (((1,), (1,)), ((), ())), preferred_element_type=jnp.float32)
 
@@ -126,24 +122,25 @@
 def fused(
     groups,
     lanes,
-    tok_ref,
-    cot_ref,
     routes_ref,
     probs_ref,
+    tok_hbm,
+    cot_hbm,
     wg_hbm,
     wu_hbm,
     wd_hbm,
     tg_ref,
     pg_ref,
-    gg_hbm,
-    ug_hbm,
-    dg_hbm,
+    tok_t_ref,
+    sc_t_ref,
+    cot_rows_ref,
+    d_gate_ref,
+    d_up_ref,
+    tok_ref,
+    cot_ref,
     wg,
     wu,
     wd,
-    gg,
-    ug,
-    dg,
     send_a,
     recv_a,
     send_rs,
@@ -152,7 +149,6 @@
     send_b,
     recv_b,
     win_sem,
-    wout_sem,
     sa_sem,
     ra_sem,
     ss_sem,
@@ -166,7 +162,7 @@
     g_me = lax.axis_index("grp")
     l_me = lax.axis_index("lane")
     tok_rows, width = tok_ref.shape
-    fanout = routes_ref.shape[1]
+    fanout = routes_ref.shape[0]
     units = wg.shape[1]
     chunk = units // lanes
     rows = groups * MOST
@@ -180,12 +176,16 @@
     for l in lane_peers:
         pl.semaphore_signal(barrier, inc=1, device_id=(g_me, l), device_id_type=MESH)
 
+    first = [
+        pltpu.make_async_copy(tok_hbm, tok_ref, win_sem.at[3]),
+        pltpu.make_async_copy(cot_hbm, cot_ref, win_sem.at[4]),
+    ]
     loads = [
         pltpu.make_async_copy(wg_hbm.at[0], wg, win_sem.at[0]),
         pltpu.make_async_copy(wu_hbm.at[0], wu, win_sem.at[1]),
         pltpu.make_async_copy(wd_hbm.at[0], wd, win_sem.at[2]),
     ]
-    for load in loads:
+    for load in first + loads:
         load.start()
 
     r_wide = routes_ref[...]
@@ -202,10 +202,9 @@
     named_t = jnp.zeros((tok_rows, rows), f32)
     hits = []
     for k in range(fanout):
-        r_col = r_wide[:, k : k + 1].astype(f32)
-        p_col = p_wide[:, k : k + 1]
-        r_lane = jnp.sum(jnp.where(eye, r_col, 0.0), axis=0, keepdims=True)
-        p_lane = jnp.sum(jnp.where(eye, p_col, 0.0), axis=0, keepdims=True)
+        r_lane = r_wide[k : k + 1].astype(f32)
+        p_lane = p_wide[k : k + 1]
+        r_col = jnp.sum(jnp.where(eye, r_lane, 0.0), axis=1, keepdims=True)
         hit = (row_exp.astype(f32) == r_lane).astype(f32)
         named = named + hit
         chance = chance + hit * p_lane
@@ -222,6 +221,8 @@
     placer_t = jnp.where(before_t == col_slot.astype(f32), named_t, 0.0)
     row_prob = jnp.sum(placer * chance, axis=1, keepdims=True)
     placed = placer.astype(bf16)
+    for load in first:
+        load.wait()
     out_tok = jnp.dot(placed, tok_ref[...], preferred_element_type=f32)
     out_cot = jnp.dot(placed, cot_ref[...], preferred_element_type=f32)
     prob_tile = jnp.broadcast_to(row_prob, (rows, chunk))
@@ -356,17 +357,11 @@
         b_copy(g, g_me).start()
     recv_b[g_me] = send_b[g_me]
 
-    stores = [
-        pltpu.make_async_copy(gg, gg_hbm.at[0], wout_sem.at[0]),
-        pltpu.make_async_copy(ug, ug_hbm.at[0], wout_sem.at[1]),
-        pltpu.make_async_copy(dg, dg_hbm.at[0], wout_sem.at[2]),
-    ]
-    gg[...] = tn_dot(rows_tok, d_gate).astype(bf16)
-    stores[0].start()
-    ug[...] = tn_dot(rows_tok, d_up).astype(bf16)
-    stores[1].start()
-    dg[...] = tn_dot(scaled, rows_cot).astype(bf16)
-    stores[2].start()
+    tok_t_ref[...] = rows_tok.astype(f32).T.astype(bf16)
+    sc_t_ref[...] = scaled.astype(f32).T.astype(bf16)
+    cot_rows_ref[...] = rows_cot
+    d_gate_ref[...] = d_gate
+    d_up_ref[...] = d_up
 
     for g in grp_peers:
         b_copy(g, g).wait_recv()
@@ -383,12 +378,10 @@
         back, top[:, : width - left], preferred_element_type=f32
     ).astype(bf16)
     dback = top[:, width - left : width - left + 128]
-    pick = lax.broadcasted_iota(jnp.int32, (tok_rows, 128), 1)
-    result = jnp.zeros((tok_rows, 128), f32)
     for k in range(fanout):
         mine = jnp.dot((placer_t * hits[k]).astype(bf16), dback, preferred_element_type=f32)
-        result = jnp.where(pick == k, mine, result)
-    pg_ref[...] = result[:, :fanout].astype(bf16)
+        lane_row = jnp.sum(jnp.where(eye, mine[:, :1], 0.0), axis=0, keepdims=True)
+        pg_ref[k : k + 1, :] = lane_row
 
     for g in grp_peers:
         a_copy(g, g_me).wait_send()
@@ -396,8 +389,19 @@
     for l in lane_peers:
         rs_copy(l, l_me).wait_send()
         ag_copy(l, l_me).wait_send()
-    for store in stores:
-        store.wait()
+
+
+def outer(tg_in, pg_in, tok_t, sc_t, cot_rows, d_gate, d_up, tg, pg, gg, ug, dg):
+    f32, bf16 = jnp.float32, jnp.bfloat16
+
+    @pl.when(pl.program_id(0) == 0)
+    def _():
+        tg[...] = tg_in[...]
+        pg[...] = pg_in[...].astype(bf16)
+
+    gg[0] = jnp.dot(tok_t[...], d_gate[...], preferred_element_type=f32).astype(bf16)
+    ug[0] = jnp.dot(tok_t[...], d_up[...], preferred_element_type=f32).astype(bf16)
+    dg[0] = jnp.dot(sc_t[...], cot_rows[...], preferred_element_type=f32).astype(bf16)
 
 
 def shards(tokens, grad_out, routes, route_probs, gate_weight, up_weight, down_weight):
@@ -413,23 +417,25 @@
     left = 128 * ((width // 128 + 2) // 2)
     bf16 = jnp.bfloat16
     vmem = pl.BlockSpec(memory_space=pltpu.VMEM)
-    hbm = pl.BlockSpec(memory_space=pl.ANY)
+    hbm = pl.BlockSpec(memory_space=pltpu.HBM)
     dma = pltpu.SemaphoreType.DMA
-    return pl.pallas_call(
+    fanout = routes.shape[1]
+    token_grad, prob_grad, tok_t, sc_t, cot_rows, d_gate, d_up = pl.pallas_call(
         functools.partial(fused, groups, lanes),
         out_shape=(
             jax.ShapeDtypeStruct(tokens.shape, bf16),
-            jax.ShapeDtypeStruct(route_probs.shape, bf16),
-            jax.ShapeDtypeStruct(gate_weight.shape, bf16),
-            jax.ShapeDtypeStruct(up_weight.shape, bf16),
-            jax.ShapeDtypeStruct(down_weight.shape, bf16),
-        ),
-        in_specs=[vmem] * 4 + [hbm] * 3,
-        out_specs=(vmem, vmem, hbm, hbm, hbm),
+            jax.ShapeDtypeStruct((fanout, tok_rows), jnp.float32),
+            jax.ShapeDtypeStruct((width, rows), bf16),
+            jax.ShapeDtypeStruct((units, rows), bf16),
+            jax.ShapeDtypeStruct((rows, width), bf16),
+            jax.ShapeDtypeStruct((rows, units), bf16),
+            jax.ShapeDtypeStruct((rows, units), bf16),
+        ),
+        in_specs=[vmem] * 2 + [hbm] * 5,
+        out_specs=(vmem,) * 7,
         scratch_shapes=[
-            pltpu.VMEM((width, units), bf16),
-            pltpu.VMEM((width, units), bf16),
-            pltpu.VMEM((units, width), bf16),
+            pltpu.VMEM((tok_rows, width), bf16),
+            pltpu.VMEM((tok_rows, width), bf16),
             pltpu.VMEM((width, units), bf16),
             pltpu.VMEM((width, units), bf16),
             pltpu.VMEM((units, width), bf16),
@@ -440,8 +446,7 @@
             pltpu.VMEM((lanes, rows, 4 * chunk), bf16),
             pltpu.VMEM((groups, 2 * MOST, left), bf16),
             pltpu.VMEM((groups, 2 * MOST, left), bf16),
-            dma((3,)),
-            dma((3,)),
+            dma((5,)),
             dma((groups,)),
             dma((groups,)),
             dma((lanes,)),
@@ -452,9 +457,41 @@
             dma((groups,)),
         ],
         compiler_params=pltpu.CompilerParams(
-            collective_id=0, has_side_effects=True, vmem_limit_bytes=48 * 1024 * 1024
-        ),
-    )(*args)
+            collective_id=0, has_side_effects=True, vmem_limit_bytes=58 * 1024 * 1024
+        ),
+    )(routes.T, route_probs.T, tokens, grad_out, gate_weight, up_weight, down_weight)
+    steps = 4
+    wide, tall = units // steps, units // steps
+    whole = lambda *shape: pl.BlockSpec(shape, lambda i: (0,) * len(shape))
+    token_grad, prob_grad, gate_grad, up_grad, down_grad = pl.pallas_call(
+        outer,
+        grid=(steps,),
+        out_shape=(
+            jax.ShapeDtypeStruct(tokens.shape, bf16),
+            jax.ShapeDtypeStruct((fanout, tok_rows), bf16),
+            jax.ShapeDtypeStruct(gate_weight.shape, bf16),
+            jax.ShapeDtypeStruct(up_weight.shape, bf16),
+            jax.ShapeDtypeStruct(down_weight.shape, bf16),
+        ),
+        in_specs=[
+            whole(tok_rows, width),
+            whole(fanout, tok_rows),
+            whole(width, rows),
+            pl.BlockSpec((tall, rows), lambda i: (i, 0)),
+            whole(rows, width),
+            pl.BlockSpec((rows, wide), lambda i: (0, i)),
+            pl.BlockSpec((rows, wide), lambda i: (0, i)),
+        ],
+        out_specs=(
+            whole(tok_rows, width),
+            whole(fanout, tok_rows),
+            pl.BlockSpec((1, width, wide), lambda i: (0, 0, i)),
+            pl.BlockSpec((1, width, wide), lambda i: (0, 0, i)),
+            pl.BlockSpec((1, tall, width), lambda i: (0, i, 0)),
+        ),
+        compiler_params=pltpu.CompilerParams(vmem_limit_bytes=58 * 1024 * 1024),
+    )(token_grad, prob_grad, tok_t, sc_t, cot_rows, d_gate, d_up)
+    return token_grad, prob_grad.T, gate_grad, up_grad, down_grad
 
 
 def solution(mesh):

time: 38.1 us -> 32.4 us (0.85)
  local copies, waits for them, and re-layouts: 12.1 us -> 0 us
  Pallas kernels: 25 us -> 31.5 us
    unnamed x16 -> x0, local copies, waits for them, and re-layouts: 11.5 us -> none
    pallas_call x0 -> x1, Pallas kernels: none -> 4.84 us  [shards(): pl.pallas_call(outer, grid=(steps,), out_shape=(jax.ShapeDtypeStruct(toke...]
    pallas_call x1, Pallas kernels: 25 us -> 26.7 us  [shards(): pl.pallas_call(functools.partial(fused, groups, lanes), out_shape=(jax.Sh...]
    pallas_call x1 -> x0, local copies, waits for them, and re-layouts: 0.6 us -> none  [shards(): pl.pallas_call(functools.partial(fused, groups, lanes), out_shape=(jax.Sh...]
where the time goes in v2:
time: 32.4 us; the launch traced here: 32.1 us
  Pallas kernels  31.5 us (97%)
  between operations  0.64 us (2%)
    pallas_call x1, Pallas kernels, shards(): pl.pallas_call(functools.partial(fused, groups, lanes), out_shape=(jax.Sh...  26.7 us
    pallas_call x1, Pallas kernels, shards(): pl.pallas_call(outer, grid=(steps,), out_shape=(jax.ShapeDtypeStruct(toke...  4.84 us

profile of v2, /device:TPU:0, one launch (start us, length us, event | category | flops | bytes accessed | tf_op | source)
XLA Modules:
  0.0 32.1 jit_solution(3846014960770675614)
XLA Ops:
  0.6 26.7 %shard_map.110 = (bf16[16,896]{1,0:T(8,128)(2,1)}, f32[2,16]{1,0:T(2,128)}, bf16[896,32]{1,0:T(8,128)(2,1)}, bf16[1024,32]{1,0:T(8,128)(2,1)}, bf16[32,896]{1,0:...) custom-call(s32[2,16]{1,0:T(2,128)} %bitcast.3, bf16[2,16]{1,0:T(2,128)(2,1)} %bitcast.4, ...), custom_call_target="tpu_custom_call" | custom-call | tf_op jit(solution)/shard_map/pallas_call | solution.py:423
  27.3 4.8 %shard_map.111 = (bf16[16,896]{1,0:T(8,128)(2,1)}, bf16[2,16]{1,0:T(2,128)(2,1)}, bf16[1,896,1024]{2,1,0:T(8,128)(2,1)}, bf16[1,896,1024]{2,1,0:T(8,128)(2,1)}, bf16[1,1024,896]{2,1,0:T(8,128)(2,1)}) custom-call(bf16[16,896]{1,0:T(8,128)(2,1)} %get-tuple-element.17.tg_in, f32[2,16]{1,0:T(2,128)} %get-tuple-element.18.pg_in, ...), custom_call_target="tpu_custom_call" | custom-call | tf_op jit(solution)/shard_map/pallas_call | solution.py:466

commit v3 on v2

--- a/solution.py
+++ b/solution.py
@@ -146,6 +146,7 @@
     send_rs,
     recv_rs,
     gat,
+    late,
     send_b,
     recv_b,
     win_sem,
@@ -155,6 +156,8 @@
     rs_sem,
     sg_sem,
     rg_sem,
+    sl_sem,
+    rl_sem,
     sb_sem,
     rb_sem,
 ):
@@ -304,37 +307,54 @@
     dpart = jnp.sum(hidden * grad, axis=1, keepdims=True)
     dhid = prob * grad
     gat[l_me, :, :chunk] = (dhid * upward * slope).astype(bf16)
-    gat[l_me, :, chunk : 2 * chunk] = (dhid * act).astype(bf16)
-    gat[l_me, :, 2 * chunk : 3 * chunk] = (prob * hidden).astype(bf16)
+    gat[l_me, :, chunk:] = (dhid * act).astype(bf16)
+    late[l_me, :, :chunk] = (prob * hidden).astype(bf16)
     high = dpart.astype(bf16).astype(f32)
     lane_id = lax.broadcasted_iota(jnp.int32, (rows, chunk), 1)
-    gat[l_me, :, 3 * chunk :] = jnp.where(lane_id < chunk // 2, high, dpart - high).astype(bf16)
-
-    def ag_copy(to, slot):
+    late[l_me, :, chunk:] = jnp.where(lane_id < chunk // 2, high, dpart - high).astype(bf16)
+
+    def ag_copy(buf, sent, got, to, slot):
         return pltpu.make_async_remote_copy(
-            src_ref=gat.at[slot],
-            dst_ref=gat.at[slot],
-            send_sem=sg_sem.at[to],
-            recv_sem=rg_sem.at[slot],
+            src_ref=buf.at[slot],
+            dst_ref=buf.at[slot],
+            send_sem=sent.at[to],
+            recv_sem=got.at[slot],
             device_id=(g_me, to),
             device_id_type=MESH,
         )
 
     for l in lane_peers:
-        ag_copy(l, l_me).start()
+        ag_copy(gat, sg_sem, rg_sem, l, l_me).start()
     for l in lane_peers:
-        ag_copy(l, l).wait_recv()
-
+        ag_copy(late, sl_sem, rl_sem, l, l_me).start()
+
+    contrib = jnp.zeros((rows, width), f32)
+    for j in range(chips):
+        chip = lax.rem(chip_me + j, chips)
+        if j == 0:
+            mate = 2 * chip_me + 1 - core_me
+            ag_copy(gat, sg_sem, rg_sem, mate, mate).wait_recv()
+        else:
+            for h in range(2):
+                l = 2 * chip + h
+                ag_copy(gat, sg_sem, rg_sem, l, l).wait_recv()
+        at = pl.ds(pl.multiple_of(chip * (2 * chunk), 2 * chunk), 2 * chunk)
+        one, two = gat[2 * chip], gat[2 * chip + 1]
+        pair_gate = jnp.concatenate((one[:, :chunk], two[:, :chunk]), axis=1)
+        pair_up = jnp.concatenate((one[:, chunk:], two[:, chunk:]), axis=1)
+        contrib = contrib + nt_dot(pair_gate, wg[:, at]) + nt_dot(pair_up, wu[:, at])
+
+    for l in lane_peers:
+        ag_copy(late, sl_sem, rl_sem, l, l).wait_recv()
     d_gate = jnp.concatenate([gat[l, :, :chunk] for l in range(lanes)], axis=1)
-    d_up = jnp.concatenate([gat[l, :, chunk : 2 * chunk] for l in range(lanes)], axis=1)
-    scaled = jnp.concatenate([gat[l, :, 2 * chunk : 3 * chunk] for l in range(lanes)], axis=1)
-    dtile = gat[0, :, 3 * chunk :].astype(f32)
+    d_up = jnp.concatenate([gat[l, :, chunk:] for l in range(lanes)], axis=1)
+    scaled = jnp.concatenate([late[l, :, :chunk] for l in range(lanes)], axis=1)
+    dtile = late[0, :, chunk:].astype(f32)
     for l in range(1, lanes):
-        dtile = dtile + gat[l, :, 3 * chunk :].astype(f32)
+        dtile = dtile + late[l, :, chunk:].astype(f32)
     dprob = jnp.sum(dtile, axis=1, keepdims=True) * (2.0 / chunk)
     dprob = jnp.broadcast_to(dprob, (rows, 128))
 
-    contrib = nt_dot(d_gate, wg[...]) + nt_dot(d_up, wu[...])
     for e in range(groups):
         at = slice(e * MOST, (e + 1) * MOST)
         right = jnp.concatenate((contrib[at, left:], dprob[at]), axis=1)
@@ -388,7 +408,8 @@
         b_copy(g, g_me).wait_send()
     for l in lane_peers:
         rs_copy(l, l_me).wait_send()
-        ag_copy(l, l_me).wait_send()
+        ag_copy(gat, sg_sem, rg_sem, l, l_me).wait_send()
+        ag_copy(late, sl_sem, rl_sem, l, l_me).wait_send()
 
 
 def outer(tg_in, pg_in, tok_t, sc_t, cot_rows, d_gate, d_up, tg, pg, gg, ug, dg):
@@ -443,12 +464,15 @@
             pltpu.VMEM((groups, 2 * MOST, width + chunk), bf16),
             pltpu.VMEM((lanes, rows, 3 * chunk), bf16),
             pltpu.VMEM((lanes, rows, 3 * chunk), bf16),
-            pltpu.VMEM((lanes, rows, 4 * chunk), bf16),
+            pltpu.VMEM((lanes, rows, 2 * chunk), bf16),
+            pltpu.VMEM((lanes, rows, 2 * chunk), bf16),
             pltpu.VMEM((groups, 2 * MOST, left), bf16),
             pltpu.VMEM((groups, 2 * MOST, left), bf16),
             dma((5,)),
             dma((groups,)),
             dma((groups,)),
+            dma((lanes,)),
+            dma((lanes,)),
             dma((lanes,)),
             dma((lanes,)),
             dma((lanes,)),

time: 32.4 us -> 32.2 us (level)
  no operation moved by 1% of the time
where the time goes in v3:
time: 32.2 us; the launch traced here: 31.9 us
  Pallas kernels  31.2 us (97%)
  between operations  0.64 us (2%)
    pallas_call x1, Pallas kernels, shards(): pl.pallas_call(functools.partial(fused, groups, lanes), out_shape=(jax.Sh...  26.4 us
    pallas_call x1, Pallas kernels, shards(): pl.pallas_call(outer, grid=(steps,), out_shape=(jax.ShapeDtypeStruct(toke...  4.83 us

profile of v3, /device:TPU:0, one launch (start us, length us, event | category | flops | bytes accessed | tf_op | source)
XLA Modules:
  0.0 31.9 jit_solution(1525829733175740409)
XLA Ops:
  0.6 26.4 %shard_map.110 = (bf16[16,896]{1,0:T(8,128)(2,1)}, f32[2,16]{1,0:T(2,128)}, bf16[896,32]{1,0:T(8,128)(2,1)}, bf16[1024,32]{1,0:T(8,128)(2,1)}, bf16[32,896]{1,0:...) custom-call(s32[2,16]{1,0:T(2,128)} %bitcast.3, bf16[2,16]{1,0:T(2,128)(2,1)} %bitcast.4, ...), custom_call_target="tpu_custom_call" | custom-call | tf_op jit(solution)/shard_map/pallas_call | solution.py:444
  27.1 4.8 %shard_map.111 = (bf16[16,896]{1,0:T(8,128)(2,1)}, bf16[2,16]{1,0:T(2,128)(2,1)}, bf16[1,896,1024]{2,1,0:T(8,128)(2,1)}, bf16[1,896,1024]{2,1,0:T(8,128)(2,1)}, bf16[1,1024,896]{2,1,0:T(8,128)(2,1)}) custom-call(bf16[16,896]{1,0:T(8,128)(2,1)} %get-tuple-element.17.tg_in, f32[2,16]{1,0:T(2,128)} %get-tuple-element.18.pg_in, ...), custom_call_target="tpu_custom_call" | custom-call | tf_op jit(solution)/shard_map/pallas_call | solution.py:490
